TPU v7x, 512 devices: a whole 4x8x8 slice. The times are simulated.
512 devices in a mesh: blk: 32 (over z_hi, y, core), row: 16 (over x, z_lo).
Axes of the slice: x: 4, y: 8, z: 8 (z_hi: 2, z_lo: 4; z = z_hi * 4 + z_lo), core: 2. Of those that a mesh axis runs over, the one named last changes fastest.
Arguments:
- image: bfloat16 [49152, 1152], P(('blk', 'row')), may hold values from -0.1796875 to 0.1796875
- text: bfloat16 [49152, 1152], P(('blk', 'row')), may hold values from -0.1796875 to 0.1796875
- positive: int32 [49152], P(('blk', 'row')), may hold values from 0 to 1535
- plan: int32 [2, 32], replicated, may hold values from 0 to 31, as said below
- logit_scale: float32 [1], replicated, may hold values from 4 to 16
- logit_bias: float32 [1], replicated, may hold values from -4 to -1.5
Outputs:
- grad_image: bfloat16 [49152, 1152], P(('blk', 'row'))
- grad_text: bfloat16 [49152, 1152], P(('blk', 'row'))
Inputs may be any that keep to these rules, and one draw needn't show every extreme that they name: plan[k, i] = i XOR m_k, where the 2 masks m_k are distinct and nonzero.
All inputs are finite; a program needn't handle non-finite values.
Results may differ from a plain program's by a relative error of at most 0.025.
Values may be sent and summed in bfloat16 or wider, within the bound.
A program may use at most 64 MiB of HBM per device.

v0:
```python
import jax
import jax.numpy as jnp
from jax import lax
from jax.experimental import pallas as pl
from jax.experimental.pallas import tpu as pltpu
from jax.sharding import PartitionSpec as P

MESH = pl.DeviceIdType.MESH
VMEM = pl.BlockSpec(memory_space=pltpu.VMEM)
SMEM = pl.BlockSpec(memory_space=pltpu.SMEM)
SIDE = 4
ROWS = 96
HALF = 48
TILE = SIDE * ROWS
WIDTH = 1152


def place():
    row = lax.axis_index("row")
    return lax.div(row, SIDE), lax.rem(row, SIDE)


def device(x, z):
    return {"row": lax.rem(x, SIDE) * SIDE + z}


def remote(src, dst, send, recv, index, target):
    return pltpu.make_async_remote_copy(
        src_ref=src,
        dst_ref=dst,
        send_sem=send.at[index],
        recv_sem=recv.at[index],
        device_id=target,
        device_id_type=MESH,
    )


def greet(offsets):
    x, z = place()
    barrier = pltpu.get_barrier_semaphore()

    def signal(target):
        pl.semaphore_signal(barrier, inc=1, device_id=target, device_id_type=MESH)

    for offset in offsets:
        signal(device(x + offset, z))

    @pl.when(z < SIDE - 1)
    def _():
        signal(device(x, z + 1))

    @pl.when(z > 0)
    def _():
        signal(device(x, z - 1))

    ends = jnp.where(z < SIDE - 1, 1, 0) + jnp.where(z > 0, 1, 0)
    pl.semaphore_wait(barrier, len(offsets) + ends)


def rows_of(lane):
    return pl.ds(pl.multiple_of(lane * HALF, 16), HALF)


class Ring:
    def lanes(self, step):
        @pl.loop(0, 2)
        def _(lane):
            step(lane)

    def ends(self, lane):
        sign = 1 - 2 * lane
        after = lax.rem(self.x + sign + SIDE, SIDE)
        before = lax.rem(self.x - sign + SIDE, SIDE)
        return after, before, device(after, self.z)

    def start(self):
        self.lanes(lambda lane: self.first(lane).start())
        self.lanes(lambda lane: self.second(lane).start())

    def drain(self):
        def step(lane):
            self.second(lane).wait_recv()
            self.onward(lane).wait_recv()
            for copy in (self.first, self.second, self.onward):
                copy(lane).wait_send()

        self.lanes(step)


class RingGather(Ring):
    def __init__(self, src, dst, send, recv, base):
        self.src, self.dst, self.sems = src, dst, (send, recv)
        self.base = base
        self.x, self.z = place()

    def copy(self, source, slot, rows, index, target):
        return remote(source.at[rows], self.dst.at[slot, rows], *self.sems, self.base + index, target)

    def first(self, lane):
        return self.copy(self.src, self.x, rows_of(lane), lane, self.ends(lane)[2])

    def second(self, lane):
        return self.copy(self.src, self.x, rows_of(1 - lane), 2 + lane, self.ends(lane)[2])

    def onward(self, lane):
        _, before, target = self.ends(lane)
        return self.copy(self.dst.at[before], before, rows_of(lane), 4 + lane, target)

    def forward(self):
        def step(lane):
            self.first(lane).wait_recv()
            self.onward(lane).start()

        self.lanes(step)

    def finish(self):
        self.drain()


class ChainGather:
    def __init__(self, src, dst, send, recv, base):
        self.refs = (src, dst, send, recv, base)
        self.x, self.z = place()

    def copy(self, step, lane, own=False):
        src, dst, send, recv, base = self.refs
        sign = 1 - 2 * lane
        slot = self.z - sign * step
        source = src if own else dst.at[slot]
        target = device(self.x, self.z + sign)
        return remote(source, dst.at[slot], send, recv, base + step + 3 * lane, target)

    def sends(self, step, lane):
        edge = self.z + 1 - 2 * lane
        first = self.z - (1 - 2 * lane) * step
        return (first >= 0) & (first < SIDE) & (edge >= 0) & (edge < SIDE) & (step < SIDE - 1)

    def gets(self, step, lane):
        first = self.z - (1 - 2 * lane) * (step + 1)
        return (first >= 0) & (first < SIDE)

    def start(self):
        @pl.loop(0, 2)
        def _(lane):
            @pl.when(self.sends(0, lane))
            def _():
                self.copy(0, lane, True).start()

    def forward(self, step):
        @pl.loop(0, 2)
        def _(lane):
            @pl.when(self.gets(step, lane))
            def _():
                self.copy(step, lane).wait_recv()

            @pl.when(self.sends(step + 1, lane))
            def _():
                self.copy(step + 1, lane).start()

    def finish(self):
        @pl.loop(0, 2 * (SIDE - 1))
        def _(i):
            step, lane = lax.div(i, 2), lax.rem(i, 2)

            @pl.when(self.sends(step, lane))
            def _():
                self.copy(step, lane).wait_send()


def add(out, *terms):
    @pl.loop(0, out.shape[0] // 16)
    def _(i):
        rows = pl.ds(pl.multiple_of(i * 16, 16), 16)
        total = terms[0][rows].astype(jnp.float32)
        for term in terms[1:]:
            total = total + term[rows].astype(jnp.float32)
        out[rows] = total.astype(out.dtype)


class RingSum(Ring):
    def __init__(self, part, relay, out, inbox, send, recv, base):
        self.x, self.z = place()
        self.part, self.relay, self.out, self.inbox = part, relay, out, inbox
        self.sems, self.base = (send, recv), base

    def first(self, lane):
        across = lax.rem(self.x + 2, SIDE)
        source = self.part.at[across, rows_of(lane)]
        return remote(source, self.relay.at[lane], *self.sems, self.base + lane, self.ends(lane)[2])

    def second(self, lane):
        after, _, target = self.ends(lane)
        rows = rows_of(1 - lane)
        source, into = self.part.at[after, rows], self.inbox.at[lane, rows]
        return remote(source, into, *self.sems, self.base + 2 + lane, target)

    def onward(self, lane):
        into = self.inbox.at[lane, rows_of(lane)]
        index, target = self.base + 4 + lane, self.ends(lane)[2]
        return remote(self.out.at[lane], into, *self.sems, index, target)

    def forward(self):
        def step(lane):
            self.first(lane).wait_recv()
            after = self.ends(lane)[0]
            add(self.out.at[lane], self.part.at[after, rows_of(lane)], self.relay.at[lane])
            self.onward(lane).start()

        self.lanes(step)

    def finish(self, total):
        self.drain()
        add(total, self.part.at[self.x], self.inbox.at[0], self.inbox.at[1])


RING_SUM = [
    pltpu.VMEM((3, 2, HALF, WIDTH), jnp.bfloat16),
    pltpu.VMEM((3, 2, HALF, WIDTH), jnp.bfloat16),
    pltpu.VMEM((3, 2, ROWS, WIDTH), jnp.bfloat16),
]


class ChainSum:
    def __init__(self, part, out, inbox, send, recv, base):
        self.refs = (part, out, inbox, send, recv, base)
        self.x, self.z = place()

    def copy(self, step, lane, own=False):
        part, out, inbox, send, recv, base = self.refs
        source = part.at[self.slot(step, lane)] if own else out.at[lane, step]
        target = device(self.x, self.z + 1 - 2 * lane)
        return remote(source, inbox.at[lane, step], send, recv, base + step + 3 * lane, target)

    def slot(self, step, lane):
        return jnp.where(lane == 0, SIDE - 1 - step, step)

    def sends(self, step, lane):
        slot = self.slot(step, lane)
        return ((lane == 0) & (self.z < slot)) | ((lane == 1) & (self.z > slot))

    def fed(self, lane):
        return ((lane == 0) & (self.z > 0)) | ((lane == 1) & (self.z < SIDE - 1))

    def start(self):
        @pl.loop(0, 2 * (SIDE - 1))
        def _(i):
            step, lane = lax.div(i, 2), lax.rem(i, 2)

            @pl.when(self.sends(step, lane) & jnp.logical_not(self.fed(lane)))
            def _():
                self.copy(step, lane, True).start()

    def forward(self, step):
        part, out, inbox = self.refs[:3]

        @pl.loop(0, 2)
        def _(i):
            lane = lax.rem(i + lax.div(self.z, 2), 2)

            @pl.when(self.sends(step, lane) & self.fed(lane))
            def _():
                self.copy(step, lane).wait_recv()
                add(out.at[lane, step], part.at[self.slot(step, lane)], inbox.at[lane, step])
                self.copy(step, lane).start()

    def finish(self, total):
        part, out, inbox = self.refs[:3]
        add(total, part.at[self.z])

        @pl.loop(0, 2)
        def _(lane):
            step = jnp.where(lane == 0, SIDE - 1 - self.z, self.z)

            @pl.when(self.fed(lane))
            def _():
                self.copy(step, lane).wait_recv()
                add(total, total, inbox.at[lane, step])

        @pl.loop(0, 2 * (SIDE - 1))
        def _(i):
            step, lane = lax.div(i, 2), lax.rem(i, 2)

            @pl.when(self.sends(step, lane))
            def _():
                self.copy(step, lane).wait_send()


CHAIN_SUM = [
    pltpu.VMEM((2, SIDE - 1, ROWS, WIDTH), jnp.bfloat16),
    pltpu.VMEM((2, SIDE - 1, ROWS, WIDTH), jnp.bfloat16),
]


def semaphores(count):
    return [pltpu.SemaphoreType.DMA((count,)), pltpu.SemaphoreType.DMA((count,))]


def call(kernel, name, number, out, scratch, flops=0, specs=None):
    def run(*args):
        return pl.pallas_call(
            kernel,
            out_shape=out,
            in_specs=specs or [VMEM] * len(args),
            out_specs=jax.tree.map(lambda _: VMEM, out),
            scratch_shapes=scratch,
            compiler_params=pltpu.CompilerParams(
                collective_id=number,
                has_side_effects=number is not None,
                vmem_limit_bytes=48 * 2**20,
            ),
            cost_estimate=pl.CostEstimate(flops=flops, bytes_accessed=2**25, transcendentals=0),
            name=name,
        )(*args)

    return run


def bf16(*shape):
    return jax.ShapeDtypeStruct(shape, jnp.bfloat16)


def f32(*shape):
    return jax.ShapeDtypeStruct(shape, jnp.float32)


def keep(src, dst, sem):
    copy = pltpu.make_async_copy(src, dst, sem)
    copy.start()
    return copy


def core(scalars, text, image, one, two, positive, back_one, back_two, own_sum, text_sum, *scratch):
    texts, piles, parts, part_text, total, places = scratch[:6]
    relays, outs, inboxes, chain_out, chain_in, send, recv, local = scratch[6:]
    x, z = place()
    scale = scalars[0]
    bias = scalars[1]
    greet((1, 2, 3))
    chain = ChainGather(text, texts, send, recv, 0)
    sources = (image, one, two)
    rings = [RingGather(sources[k], piles.at[k], send, recv, 6 * k + 6) for k in range(3)]

    def hint(k):
        return remote(positive, places.at[x], send, recv, 23 + k, device(x + k, z))

    rings[0].start()
    chain.start()

    @pl.loop(1, SIDE)
    def _(k):
        hint(k).start()

    kept = [keep(text, texts.at[z], local.at[0]), keep(positive, places.at[x], local.at[1])]
    kept += [keep(sources[k], piles.at[k, x], local.at[2 + k]) for k in range(3)]
    rings[0].forward()
    rings[1].start()
    chain.forward(0)
    rings[1].forward()
    rings[2].start()
    chain.forward(1)
    rings[2].forward()
    chain.forward(2)
    chain.finish()
    for copy in kept:
        copy.wait()

    @pl.loop(1, SIDE)
    def _(k):
        hint(k).wait()

    def products(k):
        flat = piles[k].reshape(TILE, WIDTH)
        whole = texts[...].reshape(TILE, WIDTH)
        prod = lax.dot_general(
            flat, whole, (((1,), (1,)), ((), ())), preferred_element_type=jnp.float32
        )
        grad = 0.5 * jnp.tanh(0.5 * (scale * prod + bias)) + 0.5
        if k == 0:
            grad = grad - marked()
        grad = grad.astype(jnp.bfloat16)
        back = scale * jnp.dot(grad, whole, preferred_element_type=jnp.float32)
        parts[k] = back.astype(jnp.bfloat16).reshape(SIDE, ROWS, WIDTH)
        return grad, flat

    def gains(k, grad, flat):
        gain = lax.dot_general(
            grad, flat, (((0,), (0,)), ((), ())), preferred_element_type=jnp.float32
        )
        if k == 0:
            total[...] = gain
        elif k == 1:
            total[...] += gain
        else:
            gain = total[...] + gain
            part_text[...] = gain.astype(jnp.bfloat16).reshape(SIDE, ROWS, WIDTH)

    def marked():
        lanes = lax.broadcasted_iota(jnp.int32, (ROWS, ROWS), 1)
        diagonal = lax.broadcasted_iota(jnp.int32, (ROWS, ROWS), 0) == lanes
        index = (lax.broadcasted_iota(jnp.int32, (ROWS, TILE), 1) + x * TILE).astype(jnp.float32)
        marks = []
        for slot in range(SIDE):
            spots = jnp.broadcast_to(places[slot].astype(jnp.float32), (ROWS, ROWS))
            spot = jnp.sum(jnp.where(diagonal, spots, 0.0), axis=1, keepdims=True)
            marks.append(jnp.where(index == spot, 1.0, 0.0))
        return jnp.concatenate(marks, axis=0)

    sums = [
        RingSum(parts.at[k], relays.at[k], outs.at[k], inboxes.at[k], send, recv, 6 * k + 33)
        for k in range(3)
    ]
    chain = ChainSum(part_text, chain_out, chain_in, send, recv, 27)
    rings[0].finish()
    gain = products(0)
    sums[0].start()
    gains(0, *gain)
    rings[1].finish()
    gain = products(1)
    sums[1].start()
    gains(1, *gain)
    sums[0].forward()
    rings[2].finish()
    gain = products(2)
    sums[2].start()
    gains(2, *gain)
    chain.start()
    sums[1].forward()
    chain.forward(0)
    sums[2].forward()
    chain.forward(1)
    chain.forward(2)
    for ring, result in zip(sums, (own_sum, back_one, back_two)):
        ring.finish(result)
    chain.finish(text_sum)


def exchange(value, mask):
    count = lax.axis_size("blk")

    def branch(m):
        pairs = [(source, source ^ m) for source in range(count)]
        return lambda v: lax.ppermute(v, "blk", pairs)

    return lax.switch(mask - 1, [branch(m) for m in range(1, count)], value)


def unit_rows(x):
    xf = x.astype(jnp.float32)
    norm = jnp.sqrt(jnp.sum(xf * xf, axis=-1, keepdims=True) + 1e-06)
    return (xf / norm, norm)


def prepare(image, text, image_hat, text_hat):
    for source, target in ((image, image_hat), (text, text_hat)):
        target[...] = unit_rows(source[...])[0].astype(jnp.bfloat16)


def norm_backward(grad, value):
    unit, norm = unit_rows(value)
    return ((grad - unit * jnp.sum(unit * grad, axis=-1, keepdims=True)) / norm).astype(jnp.bfloat16)


def conclude(scalars, image, text, own, one, two, txt, grad_image, grad_text):
    grad = own[...].astype(jnp.float32) + one[...].astype(jnp.float32) + two[...].astype(jnp.float32)
    grad_image[...] = norm_backward(grad, image[...])
    grad_text[...] = norm_backward(scalars[0] * txt[...], text[...])


def shards(image, text, positive, plan, logit_scale, logit_bias):
    masks = plan[:, 0]
    scalars = jnp.concatenate([logit_scale, logit_bias])
    shard = bf16(ROWS, WIDTH)
    wide = f32(ROWS, WIDTH)

    img_hat, txt_hat = call(prepare, "prepare", None, (shard, shard), [])(image, text)
    fetched = [exchange(img_hat, masks[step]) for step in range(2)]
    middle = call(
        core,
        "core",
        0,
        (shard, shard, wide, wide),
        [
            pltpu.VMEM((SIDE, ROWS, WIDTH), jnp.bfloat16),
            pltpu.VMEM((3, SIDE, ROWS, WIDTH), jnp.bfloat16),
            pltpu.VMEM((3, SIDE, ROWS, WIDTH), jnp.bfloat16),
            pltpu.VMEM((SIDE, ROWS, WIDTH), jnp.bfloat16),
            pltpu.VMEM((TILE, WIDTH), jnp.float32),
            pltpu.VMEM((SIDE, 1, ROWS), jnp.int32),
            *RING_SUM,
            *CHAIN_SUM,
            *semaphores(51),
            pltpu.SemaphoreType.DMA((5,)),
        ],
        flops=18 * TILE * TILE * WIDTH,
        specs=[SMEM] + [VMEM] * 5,
    )
    back_one, back_two, own_sum, text_sum = middle(
        scalars, txt_hat, img_hat, *fetched, positive.reshape(1, ROWS)
    )
    returned = [exchange(back, masks[step]) for step, back in enumerate((back_one, back_two))]
    last = call(conclude, "conclude", None, (shard, shard), [], specs=[SMEM] + [VMEM] * 6)
    return last(scalars, image, text, own_sum, *returned, text_sum)


def solution(mesh):
    placed = (P(("blk", "row"), None), P(("blk", "row"), None), P(("blk", "row")), P(), P(), P())
    return jax.shard_map(
        shards,
        mesh=mesh,
        in_specs=placed,
        out_specs=(P(("blk", "row"), None), P(("blk", "row"), None)),
        check_vma=False,
    )
```

profile of v0, /device:TPU:9, one launch (start us, length us, event | category | flops | bytes accessed | tf_op | source)
XLA Modules:
  0.0 159.2 jit_solution(15490294121090837531)
XLA Ops:
  1.9 0.1 pad_maximum_fusion.scalars
  2.0 0.0 copy-start.5
  2.0 0.7 copy-done.5
  2.7 0.5 fusion
  4.5 0.0 copy-start
  4.5 0.9 copy-done
  5.4 0.0 copy-start.2
  5.4 0.9 copy-done.2
  6.4 0.2 prepare.1
  6.6 28.2 %conditional.5 = (bf16[96,1152]{1,0:T(8,128)(2,1)}) conditional(s32[]{:T(128)} %bitcast.1, bf16[96,1152]{1,0:T(8,128)(2,1)S(1)} %get-tuple-element.261.image, bf16[96,1152]{1,0:T(8,128)(2,1)S(1)} %get-tuple-element.261.image, bf16[96,1152]{1,0:T(8,128)(2,1)S(1)} %get-tuple-element.261.image, ...), branch_computations={%region_31.0_spmd, %region_32.0_spmd, %region_33.0_spmd, %region_3... | conditional | bytes 884784 | solution.py:444
  6.6 15.6 %collective-permute-start.55 = (bf16[96,1152]{1,0:T(8,128)(2,1)S(1)}, bf16[96,1152]{1,0:T(8,128)(2,1)}, u32[]{:S(2)}, u32[]{:S(2)}) collective-permute-start(bf16[96,1152]{1,0:T(8,128)(2,1)S(1)} %param.55), channel_id=1, source_target_pairs={{0,400},{16,384},{32,432},{48,416},{64,464},{80,448},{96,496},{112... | collective-permute-start | bytes 663560 | tf_op jit(solution)/shard_map/cond/branch_24_fun/ppermute | solution.py:442
  22.2 12.6 %collective-permute-done.55 = bf16[96,1152]{1,0:T(8,128)(2,1)} collective-permute-done((bf16[96,1152]{1,0:T(8,128)(2,1)S(1)}, bf16[96,1152]{1,0:T(8,128)(2,1)}, u32[]{:S(2)}, u32[]{:S(2)}) %collective-permute-start.55) | collective-permute-done | bytes 221216 | tf_op jit(solution)/shard_map/cond/branch_24_fun/ppermute | solution.py:442
  34.8 24.1 %conditional.4 = (bf16[96,1152]{1,0:T(8,128)(2,1)}) conditional(s32[]{:T(128)} %bitcast, bf16[96,1152]{1,0:T(8,128)(2,1)S(1)} %get-tuple-element.261.image, bf16[96,1152]{1,0:T(8,128)(2,1)S(1)} %get-tuple-element.261.image, bf16[96,1152]{1,0:T(8,128)(2,1)S(1)} %get-tuple-element.261.image, ...), branch_computations={%region_0.0_spmd, %region_1.0_spmd, %region_2.0_spmd, %region_3.0_... | conditional | bytes 884784 | solution.py:444
  34.8 12.4 %collective-permute-start.22 = (bf16[96,1152]{1,0:T(8,128)(2,1)S(1)}, bf16[96,1152]{1,0:T(8,128)(2,1)}, u32[]{:S(2)}, u32[]{:S(2)}) collective-permute-start(bf16[96,1152]{1,0:T(8,128)(2,1)S(1)} %param.22), channel_id=1, source_target_pairs={{0,368},{16,352},{32,336},{48,320},{64,304},{80,288},{96,272},{112... | collective-permute-start | bytes 663560 | tf_op jit(solution)/shard_map/cond/branch_22_fun/ppermute | solution.py:442
  47.1 11.7 %collective-permute-done.22 = bf16[96,1152]{1,0:T(8,128)(2,1)} collective-permute-done((bf16[96,1152]{1,0:T(8,128)(2,1)S(1)}, bf16[96,1152]{1,0:T(8,128)(2,1)}, u32[]{:S(2)}, u32[]{:S(2)}) %collective-permute-start.22) | collective-permute-done | bytes 221216 | tf_op jit(solution)/shard_map/cond/branch_22_fun/ppermute | solution.py:442
  58.8 0.0 copy-start.4
  58.8 0.7 copy-done.4
  59.5 0.0 copy-start.1
  59.5 0.0 copy-start.3
  59.5 48.9 %core.1 = (bf16[96,1152]{1,0:T(8,128)(2,1)S(1)}, bf16[96,1152]{1,0:T(8,128)(2,1)S(1)}, f32[96,1152]{1,0:T(8,128)S(1)}, f32[96,1152]{1,0:T(8,128)S(1)}) custom-call(f32[2]{0:T(128)S(1)} %pad_maximum_fusion.scalars, bf16[96,1152]{1,0:T(8,128)(2,1)S(1)} %get-tuple-element.260.text, bf16[96,1152]{1,0:T(8,128)(2,1)S(1)} %get-tuple-element.261.image, ...), custom_call_target="tpu_custom_call" | custom-call | flops 3057647616 | bytes 33554432 | tf_op jit(solution)/shard_map/core/pallas_call | solution.py:300
  108.4 25.9 %conditional.6 = (bf16[96,1152]{1,0:T(8,128)(2,1)}) conditional(s32[]{:T(128)} %bitcast, bf16[96,1152]{1,0:T(8,128)(2,1)S(1)} %get-tuple-element.263, bf16[96,1152]{1,0:T(8,128)(2,1)S(1)} %get-tuple-element.263, bf16[96,1152]{1,0:T(8,128)(2,1)S(1)} %get-tuple-element.263, ...), branch_computations={%region_62.0_spmd, %region_63.0_spmd, %region_64.0_spmd, %region_6... | conditional | bytes 884784 | solution.py:444
  108.5 14.1 %collective-permute-start.84 = (bf16[96,1152]{1,0:T(8,128)(2,1)S(1)}, bf16[96,1152]{1,0:T(8,128)(2,1)}, u32[]{:S(2)}, u32[]{:S(2)}) collective-permute-start(bf16[96,1152]{1,0:T(8,128)(2,1)S(1)} %param.84), channel_id=1, source_target_pairs={{0,368},{16,352},{32,336},{48,320},{64,304},{80,288},{96,272},{112... | collective-permute-start | bytes 663560 | tf_op jit(solution)/shard_map/cond/branch_22_fun/ppermute | solution.py:442
  122.6 11.8 %collective-permute-done.84 = bf16[96,1152]{1,0:T(8,128)(2,1)} collective-permute-done((bf16[96,1152]{1,0:T(8,128)(2,1)S(1)}, bf16[96,1152]{1,0:T(8,128)(2,1)}, u32[]{:S(2)}, u32[]{:S(2)}) %collective-permute-start.84) | collective-permute-done | bytes 221216 | tf_op jit(solution)/shard_map/cond/branch_22_fun/ppermute | solution.py:442
  134.4 22.7 %conditional.7 = (bf16[96,1152]{1,0:T(8,128)(2,1)}) conditional(s32[]{:T(128)} %bitcast.1, bf16[96,1152]{1,0:T(8,128)(2,1)S(1)} %get-tuple-element.264, bf16[96,1152]{1,0:T(8,128)(2,1)S(1)} %get-tuple-element.264, bf16[96,1152]{1,0:T(8,128)(2,1)S(1)} %get-tuple-element.264, ...), branch_computations={%region_93.0_spmd, %region_94.0_spmd, %region_95.0_spmd, %region_9... | conditional | bytes 884784 | solution.py:444
  134.4 2.6 %collective-permute-start.117 = (bf16[96,1152]{1,0:T(8,128)(2,1)S(1)}, bf16[96,1152]{1,0:T(8,128)(2,1)}, u32[]{:S(2)}, u32[]{:S(2)}) collective-permute-start(bf16[96,1152]{1,0:T(8,128)(2,1)S(1)} %param.117), channel_id=1, source_target_pairs={{0,400},{16,384},{32,432},{48,416},{64,464},{80,448},{96,496},{112... | collective-permute-start | bytes 663560 | tf_op jit(solution)/shard_map/cond/branch_24_fun/ppermute | solution.py:442
  137.0 20.0 %collective-permute-done.117 = bf16[96,1152]{1,0:T(8,128)(2,1)} collective-permute-done((bf16[96,1152]{1,0:T(8,128)(2,1)S(1)}, bf16[96,1152]{1,0:T(8,128)(2,1)}, u32[]{:S(2)}, u32[]{:S(2)}) %collective-permute-start.117) | collective-permute-done | bytes 221216 | tf_op jit(solution)/shard_map/cond/branch_24_fun/ppermute | solution.py:442
  157.0 0.0 copy-done.1
  157.0 0.0 copy-done.3
  157.0 2.2 %conclude.1 = (bf16[96,1152]{1,0:T(8,128)(2,1)}, bf16[96,1152]{1,0:T(8,128)(2,1)}) custom-call(f32[2]{0:T(128)S(1)} %pad_maximum_fusion.scalars, bf16[96,1152]{1,0:T(8,128)(2,1)S(1)} %copy-done.1, bf16[96,1152]{1,0:T(8,128)(2,1)S(1)} %copy-done.3, f32[96,1152]{1,0:T(8,128)S(1)} %get-tuple-element.262.own, bf16[96,1152]{1,0:T(8,128)(2,1)} %get-tuple-element.270.one, ...), custom_call_target="tpu_custom_call" | custom-call | bytes 33554432 | tf_op jit(solution)/shard_map/conclude/pallas_call | solution.py:300
Async XLA Ops:
  2.0 0.7 copy-start.5
  4.5 0.9 copy-start
  5.4 0.9 copy-start.2
  6.6 28.2 %collective-permute-start.55 = (bf16[96,1152]{1,0:T(8,128)(2,1)S(1)}, bf16[96,1152]{1,0:T(8,128)(2,1)}, u32[]{:S(2)}, u32[]{:S(2)}) collective-permute-start(bf16[96,1152]{1,0:T(8,128)(2,1)S(1)} %param.55), channel_id=1, source_target_pairs={{0,400},{16,384},{32,432},{48,416},{64,464},{80,448},{96,496},{112... | collective-permute-start | bytes 663560 | tf_op jit(solution)/shard_map/cond/branch_24_fun/ppermute | solution.py:442
  34.8 24.1 %collective-permute-start.22 = (bf16[96,1152]{1,0:T(8,128)(2,1)S(1)}, bf16[96,1152]{1,0:T(8,128)(2,1)}, u32[]{:S(2)}, u32[]{:S(2)}) collective-permute-start(bf16[96,1152]{1,0:T(8,128)(2,1)S(1)} %param.22), channel_id=1, source_target_pairs={{0,368},{16,352},{32,336},{48,320},{64,304},{80,288},{96,272},{112... | collective-permute-start | bytes 663560 | tf_op jit(solution)/shard_map/cond/branch_22_fun/ppermute | solution.py:442
  58.8 0.7 copy-start.4
  59.5 97.5 %copy-start.1 = (bf16[96,1152]{1,0:T(8,128)(2,1)S(1)}, bf16[96,1152]{1,0:T(8,128)(2,1)}, u32[]{:S(2)}) copy-start(bf16[96,1152]{1,0:T(8,128)(2,1)} %image.3) | copy-start | bytes 663556
  59.5 97.5 %copy-start.3 = (bf16[96,1152]{1,0:T(8,128)(2,1)S(1)}, bf16[96,1152]{1,0:T(8,128)(2,1)}, u32[]{:S(2)}) copy-start(bf16[96,1152]{1,0:T(8,128)(2,1)} %text.3) | copy-start | bytes 663556
  108.5 25.9 %collective-permute-start.84 = (bf16[96,1152]{1,0:T(8,128)(2,1)S(1)}, bf16[96,1152]{1,0:T(8,128)(2,1)}, u32[]{:S(2)}, u32[]{:S(2)}) collective-permute-start(bf16[96,1152]{1,0:T(8,128)(2,1)S(1)} %param.84), channel_id=1, source_target_pairs={{0,368},{16,352},{32,336},{48,320},{64,304},{80,288},{96,272},{112... | collective-permute-start | bytes 663560 | tf_op jit(solution)/shard_map/cond/branch_22_fun/ppermute | solution.py:442
  134.4 22.7 %collective-permute-start.117 = (bf16[96,1152]{1,0:T(8,128)(2,1)S(1)}, bf16[96,1152]{1,0:T(8,128)(2,1)}, u32[]{:S(2)}, u32[]{:S(2)}) collective-permute-start(bf16[96,1152]{1,0:T(8,128)(2,1)S(1)} %param.117), channel_id=1, source_target_pairs={{0,400},{16,384},{32,432},{48,416},{64,464},{80,448},{96,496},{112... | collective-permute-start | bytes 663560 | tf_op jit(solution)/shard_map/cond/branch_24_fun/ppermute | solution.py:442
where the time goes:
time: 160 us; the launch traced here: 159 us
  waiting for transfers between devices  56.1 us (35%)
  Pallas kernels  51.3 us (32%)
  starting transfers between devices  44.7 us (28%)
  local copies, waits for them, and re-layouts  3.73 us (2%)
  between operations  3.26 us (2%)
    ppermute x4, waiting for transfers between devices, branch(): return lambda v: lax.ppermute(v, 'blk', pairs)  56.1 us
    pallas_call x3, Pallas kernels, run(): pl.pallas_call(kernel, out_shape=out, in_specs=specs or [VMEM] * len(args...  51.3 us
    ppermute x4, starting transfers between devices, branch(): return lambda v: lax.ppermute(v, 'blk', pairs)  44.7 us
    unnamed x12, local copies, waits for them, and re-layouts  3.21 us
  transfers between devices with their start and end apart: 4, of which 4 were waited for; matrix products, arithmetic and copies ran while one was open for 0% of the time, Pallas kernels for 0%

commit v1 on v0

--- a/solution.py
+++ b/solution.py
@@ -214,9 +214,9 @@
 
 
 RING_SUM = [
-    pltpu.VMEM((3, 2, HALF, WIDTH), jnp.bfloat16),
-    pltpu.VMEM((3, 2, HALF, WIDTH), jnp.bfloat16),
-    pltpu.VMEM((3, 2, ROWS, WIDTH), jnp.bfloat16),
+    pltpu.VMEM((2, HALF, WIDTH), jnp.bfloat16),
+    pltpu.VMEM((2, HALF, WIDTH), jnp.bfloat16),
+    pltpu.VMEM((2, ROWS, WIDTH), jnp.bfloat16),
 ]
 
 
@@ -329,70 +329,77 @@
     return copy
 
 
-def core(scalars, text, image, one, two, positive, back_one, back_two, own_sum, text_sum, *scratch):
-    texts, piles, parts, part_text, total, places = scratch[:6]
-    relays, outs, inboxes, chain_out, chain_in, send, recv, local = scratch[6:]
+def gather(pair, images, texts, send, recv, local):
+    x, z = place()
+    greet((1, 3))
+    chain = ChainGather(pair.at[1], texts, send, recv, 0)
+    ring = RingGather(pair.at[0], images, send, recv, 6)
+    chain.start()
+    ring.start()
+    kept = [keep(pair.at[0], images.at[x], local.at[0]), keep(pair.at[1], texts.at[z], local.at[1])]
+    ring.forward()
+    for step in range(SIDE - 1):
+        chain.forward(step)
+    ring.finish()
+    chain.finish()
+    for copy in kept:
+        copy.wait()
+
+
+def core(
+    scalars,
+    own_images,
+    own_texts,
+    one_images,
+    one_texts,
+    pair,
+    positive,
+    image_sum,
+    text_sum,
+    *scratch,
+):
+    two_images, two_texts, part_image, part_text, ga, gt, places = scratch[:7]
+    relay, out, inbox, chain_out, chain_in, send, recv, local = scratch[7:]
     x, z = place()
     scale = scalars[0]
     bias = scalars[1]
     greet((1, 2, 3))
-    chain = ChainGather(text, texts, send, recv, 0)
-    sources = (image, one, two)
-    rings = [RingGather(sources[k], piles.at[k], send, recv, 6 * k + 6) for k in range(3)]
+    chain = ChainGather(pair.at[1], two_texts, send, recv, 0)
+    ring = RingGather(pair.at[0], two_images, send, recv, 6)
 
     def hint(k):
-        return remote(positive, places.at[x], send, recv, 23 + k, device(x + k, z))
-
-    rings[0].start()
-    chain.start()
+        return remote(positive, places.at[x], send, recv, 11 + k, device(x + k, z))
 
     @pl.loop(1, SIDE)
     def _(k):
         hint(k).start()
 
-    kept = [keep(text, texts.at[z], local.at[0]), keep(positive, places.at[x], local.at[1])]
-    kept += [keep(sources[k], piles.at[k, x], local.at[2 + k]) for k in range(3)]
-    rings[0].forward()
-    rings[1].start()
-    chain.forward(0)
-    rings[1].forward()
-    rings[2].start()
-    chain.forward(1)
-    rings[2].forward()
-    chain.forward(2)
-    chain.finish()
-    for copy in kept:
-        copy.wait()
-
-    @pl.loop(1, SIDE)
-    def _(k):
-        hint(k).wait()
-
-    def products(k):
-        flat = piles[k].reshape(TILE, WIDTH)
-        whole = texts[...].reshape(TILE, WIDTH)
+    ring.start()
+    chain.start()
+    kept = [
+        keep(positive, places.at[x], local.at[0]),
+        keep(pair.at[0], two_images.at[x], local.at[1]),
+        keep(pair.at[1], two_texts.at[z], local.at[2]),
+    ]
+
+    def weights(images, texts):
         prod = lax.dot_general(
-            flat, whole, (((1,), (1,)), ((), ())), preferred_element_type=jnp.float32
+            images[...].reshape(TILE, WIDTH),
+            texts[...].reshape(TILE, WIDTH),
+            (((1,), (1,)), ((), ())),
+            preferred_element_type=jnp.float32,
         )
-        grad = 0.5 * jnp.tanh(0.5 * (scale * prod + bias)) + 0.5
-        if k == 0:
-            grad = grad - marked()
-        grad = grad.astype(jnp.bfloat16)
-        back = scale * jnp.dot(grad, whole, preferred_element_type=jnp.float32)
-        parts[k] = back.astype(jnp.bfloat16).reshape(SIDE, ROWS, WIDTH)
-        return grad, flat
-
-    def gains(k, grad, flat):
-        gain = lax.dot_general(
-            grad, flat, (((0,), (0,)), ((), ())), preferred_element_type=jnp.float32
+        return 0.5 * jnp.tanh(0.5 * (scale * prod + bias)) + 0.5
+
+    def image_term(grad, texts):
+        right = texts[...].reshape(TILE, WIDTH)
+        return jnp.dot(grad, right, preferred_element_type=jnp.float32)
+
+    def text_term(grad, images):
+        right = images[...].reshape(TILE, WIDTH)
+        return lax.dot_general(
+            grad, right, (((0,), (0,)), ((), ())), preferred_element_type=jnp.float32
         )
-        if k == 0:
-            total[...] = gain
-        elif k == 1:
-            total[...] += gain
-        else:
-            gain = total[...] + gain
-            part_text[...] = gain.astype(jnp.bfloat16).reshape(SIDE, ROWS, WIDTH)
 
     def marked():
         lanes = lax.broadcasted_iota(jnp.int32, (ROWS, ROWS), 1)
@@ -405,43 +412,53 @@
             marks.append(jnp.where(index == spot, 1.0, 0.0))
         return jnp.concatenate(marks, axis=0)
 
-    sums = [
-        RingSum(parts.at[k], relays.at[k], outs.at[k], inboxes.at[k], send, recv, 6 * k + 33)
-        for k in range(3)
-    ]
-    chain = ChainSum(part_text, chain_out, chain_in, send, recv, 27)
-    rings[0].finish()
-    gain = products(0)
-    sums[0].start()
-    gains(0, *gain)
-    rings[1].finish()
-    gain = products(1)
-    sums[1].start()
-    gains(1, *gain)
-    sums[0].forward()
-    rings[2].finish()
-    gain = products(2)
-    sums[2].start()
-    gains(2, *gain)
-    chain.start()
-    sums[1].forward()
+    grad = weights(one_images, own_texts).astype(jnp.bfloat16)
+    gt[...] = text_term(grad, one_images)
+    ring.forward()
+    grad = weights(own_images, one_texts).astype(jnp.bfloat16)
+    ga[...] = image_term(grad, one_texts)
     chain.forward(0)
-    sums[2].forward()
+
+    @pl.loop(1, SIDE)
+    def _(k):
+        hint(k).wait()
+
+    for copy in kept:
+        copy.wait()
+    grad = (weights(own_images, own_texts) - marked()).astype(jnp.bfloat16)
+    gt[...] += text_term(grad, own_images)
+    ga[...] += image_term(grad, own_texts)
+    ring.finish()
+    grad = weights(two_images, own_texts).astype(jnp.bfloat16)
+    total = gt[...] + text_term(grad, two_images)
+    part_text[...] = total.astype(jnp.bfloat16).reshape(SIDE, ROWS, WIDTH)
     chain.forward(1)
+    sums = ChainSum(part_text, chain_out, chain_in, send, recv, 15)
+    sums.start()
     chain.forward(2)
-    for ring, result in zip(sums, (own_sum, back_one, back_two)):
-        ring.finish(result)
-    chain.finish(text_sum)
-
-
-def exchange(value, mask):
+    chain.finish()
+    grad = weights(own_images, two_texts).astype(jnp.bfloat16)
+    total = scale * (ga[...] + image_term(grad, two_texts))
+    part_image[...] = total.astype(jnp.bfloat16).reshape(SIDE, ROWS, WIDTH)
+    ring = RingSum(part_image, relay, out, inbox, send, recv, 21)
+    ring.start()
+    sums.forward(0)
+    ring.forward()
+    sums.forward(1)
+    sums.forward(2)
+    ring.finish(image_sum)
+    sums.finish(text_sum)
+
+
+def exchange(value, mask, beside):
     count = lax.axis_size("blk")
 
     def branch(m):
         pairs = [(source, source ^ m) for source in range(count)]
-        return lambda v: lax.ppermute(v, "blk", pairs)
-
-    return lax.switch(mask - 1, [branch(m) for m in range(1, count)], value)
+        return lambda v, w: (lax.ppermute(v, "blk", pairs), beside(w))
+
+    branches = [branch(m) for m in range(1, count)]
+    return lambda other: lax.switch(mask - 1, branches, value, other)
 
 
 def unit_rows(x):
@@ -450,9 +467,9 @@
     return (xf / norm, norm)
 
 
-def prepare(image, text, image_hat, text_hat):
-    for source, target in ((image, image_hat), (text, text_hat)):
-        target[...] = unit_rows(source[...])[0].astype(jnp.bfloat16)
+def prepare(image, text, pair):
+    for slot, source in enumerate((image, text)):
+        pair[slot] = unit_rows(source[...])[0].astype(jnp.bfloat16)
 
 
 def norm_backward(grad, value):
@@ -460,10 +477,9 @@
     return ((grad - unit * jnp.sum(unit * grad, axis=-1, keepdims=True)) / norm).astype(jnp.bfloat16)
 
 
-def conclude(scalars, image, text, own, one, two, txt, grad_image, grad_text):
-    grad = own[...].astype(jnp.float32) + one[...].astype(jnp.float32) + two[...].astype(jnp.float32)
-    grad_image[...] = norm_backward(grad, image[...])
-    grad_text[...] = norm_backward(scalars[0] * txt[...], text[...])
+def conclude(scalars, image, text, image_sum, text_sum, grad_image, grad_text):
+    grad_image[...] = norm_backward(image_sum[...], image[...])
+    grad_text[...] = norm_backward(scalars[0] * text_sum[...], text[...])
 
 
 def shards(image, text, positive, plan, logit_scale, logit_bias):
@@ -471,35 +487,37 @@
     scalars = jnp.concatenate([logit_scale, logit_bias])
     shard = bf16(ROWS, WIDTH)
     wide = f32(ROWS, WIDTH)
-
-    img_hat, txt_hat = call(prepare, "prepare", None, (shard, shard), [])(image, text)
-    fetched = [exchange(img_hat, masks[step]) for step in range(2)]
+    stack = bf16(SIDE, ROWS, WIDTH)
+    room = pltpu.VMEM((SIDE, ROWS, WIDTH), jnp.bfloat16)
+    total = pltpu.VMEM((TILE, WIDTH), jnp.float32)
+
+    own = call(prepare, "prepare", None, bf16(2, ROWS, WIDTH), [])(image, text)
+    scratch = [*semaphores(12), pltpu.SemaphoreType.DMA((2,))]
+    beside = call(gather, "gather", 0, (stack, stack), scratch)
+    one, (own_images, own_texts) = exchange(own, masks[0], beside)(own)
+    two, (one_images, one_texts) = exchange(own, masks[1], beside)(one)
     middle = call(
         core,
         "core",
-        0,
-        (shard, shard, wide, wide),
+        1,
+        (wide, wide),
         [
-            pltpu.VMEM((SIDE, ROWS, WIDTH), jnp.bfloat16),
-            pltpu.VMEM((3, SIDE, ROWS, WIDTH), jnp.bfloat16),
-            pltpu.VMEM((3, SIDE, ROWS, WIDTH), jnp.bfloat16),
-            pltpu.VMEM((SIDE, ROWS, WIDTH), jnp.bfloat16),
-            pltpu.VMEM((TILE, WIDTH), jnp.float32),
+            *[room] * 4,
+            *[total] * 2,
             pltpu.VMEM((SIDE, 1, ROWS), jnp.int32),
             *RING_SUM,
             *CHAIN_SUM,
-            *semaphores(51),
-            pltpu.SemaphoreType.DMA((5,)),
+            *semaphores(27),
+            pltpu.SemaphoreType.DMA((3,)),
         ],
-        flops=18 * TILE * TILE * WIDTH,
-        specs=[SMEM] + [VMEM] * 5,
+        flops=24 * TILE * TILE * WIDTH,
+        specs=[SMEM] + [VMEM] * 6,
     )
-    back_one, back_two, own_sum, text_sum = middle(
-        scalars, txt_hat, img_hat, *fetched, positive.reshape(1, ROWS)
+    image_sum, text_sum = middle(
+        scalars, own_images, own_texts, one_images, one_texts, two, positive.reshape(1, ROWS)
     )
-    returned = [exchange(back, masks[step]) for step, back in enumerate((back_one, back_two))]
-    last = call(conclude, "conclude", None, (shard, shard), [], specs=[SMEM] + [VMEM] * 6)
-    return last(scalars, image, text, own_sum, *returned, text_sum)
+    last = call(conclude, "conclude", None, (shard, shard), [], specs=[SMEM] + [VMEM] * 4)
+    return last(scalars, image, text, image_sum, text_sum)
 
 
 def solution(mesh):

time: 160 us -> 122 us (0.76)
  the two profiles are of different devices: /device:TPU:9 before, /device:TPU:64 now
where the time goes in v1:
time: 122 us; the launch traced here: 121 us
  Pallas kernels  96.2 us (79%)
  starting transfers between devices  17.8 us (15%)
  local copies, waits for them, and re-layouts  3.53 us (3%)
  between operations  3.29 us (3%)
    pallas_call x5, Pallas kernels, run(): pl.pallas_call(kernel, out_shape=out, in_specs=specs or [VMEM] * len(args...  96.2 us
    ppermute x2, starting transfers between devices, branch(): return lambda v, w: (lax.ppermute(v, 'blk', pairs), beside(w))  17.8 us
    unnamed x12, local copies, waits for them, and re-layouts  3.02 us
  transfers between devices with their start and end apart: 2, of which 0 were waited for; matrix products, arithmetic and copies ran while one was open for 0% of the time, Pallas kernels for 47%

profile of v1, /device:TPU:64, one launch (start us, length us, event | category | flops | bytes accessed | tf_op | source)
XLA Modules:
  0.0 121.5 jit_solution(9054853914673455207)
XLA Ops:
  0.6 0.0 copy-start
  0.6 0.9 copy-done
  1.6 0.0 copy-start.2
  1.6 0.9 copy-done.2
  2.5 0.0 copy-start.5
  2.5 0.2 prepare.1
  2.7 0.5 copy-done.5
  3.2 0.5 fusion
  4.4 49.4 %conditional.2 = (bf16[2,96,1152]{2,1,0:T(8,128)(2,1)}, bf16[4,96,1152]{2,1,0:T(8,128)(2,1)S(1)}, bf16[4,96,1152]{2,1,0:T(8,128)(2,1)S(1)}) conditional(s32[]{:T(128)} %bitcast, bf16[2,96,1152]{2,1,0:T(8,128)(2,1)S(1)} %prepare.1, bf16[2,96,1152]{2,1,0:T(8,128)(2,1)S(1)} %prepare.1, ...), branch_computations={%region_0.0_spmd, %region_1.0_spmd, %region_2.0_spmd, %region_3.0_... | conditional | bytes 35323968 | solution.py:461
  4.4 13.1 %collective-permute-start.21 = (bf16[2,96,1152]{2,1,0:T(8,128)(2,1)S(1)}, bf16[2,96,1152]{2,1,0:T(8,128)(2,1)}, u32[]{:S(2)}, u32[]{:S(2)}) collective-permute-start(bf16[2,96,1152]{2,1,0:T(8,128)(2,1)S(1)} %pair.21), channel_id=1, source_target_pairs={{0,352},{16,368},{32,320},{48,336},{64,288},{80,304},{96,256},{112... | collective-permute-start | bytes 1327112 | tf_op jit(solution)/shard_map/cond/branch_21_fun/ppermute | solution.py:458
  17.5 36.2 %gather.83 = (bf16[4,96,1152]{2,1,0:T(8,128)(2,1)S(1)}, bf16[4,96,1152]{2,1,0:T(8,128)(2,1)S(1)}) custom-call(bf16[2,96,1152]{2,1,0:T(8,128)(2,1)S(1)} %pair.21), custom_call_target="tpu_custom_call" | custom-call | bytes 33554432 | tf_op jit(solution)/shard_map/cond/branch_21_fun/gather/pallas_call | solution.py:300
  53.7 0.0 collective-permute-done.21
  54.4 26.6 %conditional.3 = (bf16[2,96,1152]{2,1,0:T(8,128)(2,1)}, bf16[4,96,1152]{2,1,0:T(8,128)(2,1)S(1)}, bf16[4,96,1152]{2,1,0:T(8,128)(2,1)}) conditional(s32[]{:T(128)} %bitcast.1, (bf16[2,96,1152]{2,1,0:T(8,128)(2,1)S(1)}, bf16[2,96,1152]{2,1,0:T(8,128)(2,1)}) %tuple.255, (bf16[2,96,1152]{2,1,0:T(8,128)(2,1)S(1)}, ...), branch_computations={%region_31.0_spmd, %region_32.0_spmd, %region_33.0_spmd, %region_3... | conditional | bytes 35323968 | solution.py:461
  54.6 4.8 %collective-permute-start.40 = (bf16[2,96,1152]{2,1,0:T(8,128)(2,1)S(1)}, bf16[2,96,1152]{2,1,0:T(8,128)(2,1)}, u32[]{:S(2)}, u32[]{:S(2)}) collective-permute-start(bf16[2,96,1152]{2,1,0:T(8,128)(2,1)S(1)} %get-tuple-element.253), channel_id=1, source_target_pairs={{0,160},{16,176},{32,128},{48,144},{64,224},{80,240},{96,192},{112... | collective-permute-start | bytes 1327112 | tf_op jit(solution)/shard_map/cond/branch_9_fun/ppermute | solution.py:458
  59.4 21.3 %gather.102 = (bf16[4,96,1152]{2,1,0:T(8,128)(2,1)S(1)}, bf16[4,96,1152]{2,1,0:T(8,128)(2,1)}) custom-call(bf16[2,96,1152]{2,1,0:T(8,128)(2,1)} %get-tuple-element.254.pair), custom_call_target="tpu_custom_call" | custom-call | bytes 33554432 | tf_op jit(solution)/shard_map/cond/branch_9_fun/gather/pallas_call | solution.py:300
  80.7 0.0 collective-permute-done.40
  82.3 0.1 pad_maximum_fusion.scalars
  82.3 0.0 copy-start.4
  82.3 0.7 copy-done.4
  83.0 0.0 copy-start.1
  83.0 0.0 copy-start.3
  83.0 36.8 %core.1 = (f32[96,1152]{1,0:T(8,128)S(1)}, f32[96,1152]{1,0:T(8,128)S(1)}) custom-call(f32[2]{0:T(128)S(1)} %pad_maximum_fusion.scalars, bf16[4,96,1152]{2,1,0:T(8,128)(2,1)S(1)} %get-tuple-element.351.own_images, bf16[4,96,1152]{2,1,0:T(8,128)(2,1)S(1)} %get-tuple-element.352.own_texts, bf16[4,96,1152]{2,1,0:T(8,128)(2,1)S(1)} %get-tuple-element.354.one_images, ...), custom_call_target="tpu_custom_call" | custom-call | flops 4076863488 | bytes 33554432 | tf_op jit(solution)/shard_map/core/pallas_call | solution.py:300
  119.8 0.0 copy-done.1
  119.9 0.0 copy-done.3
  119.9 1.6 %conclude.1 = (bf16[96,1152]{1,0:T(8,128)(2,1)}, bf16[96,1152]{1,0:T(8,128)(2,1)}) custom-call(f32[2]{0:T(128)S(1)} %pad_maximum_fusion.scalars, bf16[96,1152]{1,0:T(8,128)(2,1)S(1)} %copy-done.1, bf16[96,1152]{1,0:T(8,128)(2,1)S(1)} %copy-done.3, f32[96,1152]{1,0:T(8,128)S(1)} %get-tuple-element.357.image_sum, f32[96,1152]{1,0:T(8,128)S(1)} %get-tuple-element.358.text_sum), custom_call_target="tpu_custom_call" | custom-call | bytes 33554432 | tf_op jit(solution)/shard_map/conclude/pallas_call | solution.py:300
Async XLA Ops:
  0.6 0.9 copy-start
  1.6 0.9 copy-start.2
  2.5 0.7 copy-start.5
  4.4 49.3 %collective-permute-start.21 = (bf16[2,96,1152]{2,1,0:T(8,128)(2,1)S(1)}, bf16[2,96,1152]{2,1,0:T(8,128)(2,1)}, u32[]{:S(2)}, u32[]{:S(2)}) collective-permute-start(bf16[2,96,1152]{2,1,0:T(8,128)(2,1)S(1)} %pair.21), channel_id=1, source_target_pairs={{0,352},{16,368},{32,320},{48,336},{64,288},{80,304},{96,256},{112... | collective-permute-start | bytes 1327112 | tf_op jit(solution)/shard_map/cond/branch_21_fun/ppermute | solution.py:458
  54.6 26.1 %collective-permute-start.40 = (bf16[2,96,1152]{2,1,0:T(8,128)(2,1)S(1)}, bf16[2,96,1152]{2,1,0:T(8,128)(2,1)}, u32[]{:S(2)}, u32[]{:S(2)}) collective-permute-start(bf16[2,96,1152]{2,1,0:T(8,128)(2,1)S(1)} %get-tuple-element.253), channel_id=1, source_target_pairs={{0,160},{16,176},{32,128},{48,144},{64,224},{80,240},{96,192},{112... | collective-permute-start | bytes 1327112 | tf_op jit(solution)/shard_map/cond/branch_9_fun/ppermute | solution.py:458
  82.3 0.7 copy-start.4
  83.0 36.9 %copy-start.1 = (bf16[96,1152]{1,0:T(8,128)(2,1)S(1)}, bf16[96,1152]{1,0:T(8,128)(2,1)}, u32[]{:S(2)}) copy-start(bf16[96,1152]{1,0:T(8,128)(2,1)} %image.3) | copy-start | bytes 663556
  83.0 36.9 %copy-start.3 = (bf16[96,1152]{1,0:T(8,128)(2,1)S(1)}, bf16[96,1152]{1,0:T(8,128)(2,1)}, u32[]{:S(2)}) copy-start(bf16[96,1152]{1,0:T(8,128)(2,1)} %text.3) | copy-start | bytes 663556

commit v2 on v1

--- a/solution.py
+++ b/solution.py
@@ -57,6 +57,9 @@
     pl.semaphore_wait(barrier, len(offsets) + ends)
 
 
+HALVES = (pl.ds(0, HALF), pl.ds(HALF, HALF))
+
+
 def rows_of(lane):
     return pl.ds(pl.multiple_of(lane * HALF, 16), HALF)
 
@@ -286,8 +289,8 @@
 
 
 CHAIN_SUM = [
-    pltpu.VMEM((2, SIDE - 1, ROWS, WIDTH), jnp.bfloat16),
-    pltpu.VMEM((2, SIDE - 1, ROWS, WIDTH), jnp.bfloat16),
+    pltpu.VMEM((2, 2, SIDE - 1, HALF, WIDTH), jnp.bfloat16),
+    pltpu.VMEM((2, 2, SIDE - 1, HALF, WIDTH), jnp.bfloat16),
 ]
 
 
@@ -329,19 +332,29 @@
     return copy
 
 
+def chain_gathers(src, dst, send, recv, base):
+    return [
+        ChainGather(src.at[rows], dst.at[:, rows], send, recv, base + 6 * part)
+        for part, rows in enumerate(HALVES)
+    ]
+
+
 def gather(pair, images, texts, send, recv, local):
     x, z = place()
     greet((1, 3))
-    chain = ChainGather(pair.at[1], texts, send, recv, 0)
-    ring = RingGather(pair.at[0], images, send, recv, 6)
-    chain.start()
+    chains = chain_gathers(pair.at[1], texts, send, recv, 6)
+    ring = RingGather(pair.at[0], images, send, recv, 0)
+    for chain in chains:
+        chain.start()
     ring.start()
     kept = [keep(pair.at[0], images.at[x], local.at[0]), keep(pair.at[1], texts.at[z], local.at[1])]
     ring.forward()
     for step in range(SIDE - 1):
-        chain.forward(step)
+        for chain in chains:
+            chain.forward(step)
     ring.finish()
-    chain.finish()
+    for chain in chains:
+        chain.finish()
     for copy in kept:
         copy.wait()
 
@@ -364,18 +377,19 @@
     scale = scalars[0]
     bias = scalars[1]
     greet((1, 2, 3))
-    chain = ChainGather(pair.at[1], two_texts, send, recv, 0)
-    ring = RingGather(pair.at[0], two_images, send, recv, 6)
+    chains = chain_gathers(pair.at[1], two_texts, send, recv, 0)
+    ring = RingGather(pair.at[0], two_images, send, recv, 12)
 
     def hint(k):
-        return remote(positive, places.at[x], send, recv, 11 + k, device(x + k, z))
+        return remote(positive, places.at[x], send, recv, 17 + k, device(x + k, z))
 
     @pl.loop(1, SIDE)
     def _(k):
         hint(k).start()
 
     ring.start()
-    chain.start()
+    for chain in chains:
+        chain.start()
     kept = [
         keep(positive, places.at[x], local.at[0]),
         keep(pair.at[0], two_images.at[x], local.at[1]),
@@ -417,7 +431,8 @@
     ring.forward()
     grad = weights(own_images, one_texts).astype(jnp.bfloat16)
     ga[...] = image_term(grad, one_texts)
-    chain.forward(0)
+    for chain in chains:
+        chain.forward(0)
 
     @pl.loop(1, SIDE)
     def _(k):
@@ -432,22 +447,31 @@
     grad = weights(two_images, own_texts).astype(jnp.bfloat16)
     total = gt[...] + text_term(grad, two_images)
     part_text[...] = total.astype(jnp.bfloat16).reshape(SIDE, ROWS, WIDTH)
-    chain.forward(1)
-    sums = ChainSum(part_text, chain_out, chain_in, send, recv, 15)
-    sums.start()
-    chain.forward(2)
-    chain.finish()
+    for chain in chains:
+        chain.forward(1)
+    sums = [
+        ChainSum(part_text.at[:, rows], chain_out.at[k], chain_in.at[k], send, recv, 21 + 6 * k)
+        for k, rows in enumerate(HALVES)
+    ]
+    for total in sums:
+        total.start()
+    for chain in chains:
+        chain.forward(2)
+        chain.finish()
     grad = weights(own_images, two_texts).astype(jnp.bfloat16)
     total = scale * (ga[...] + image_term(grad, two_texts))
     part_image[...] = total.astype(jnp.bfloat16).reshape(SIDE, ROWS, WIDTH)
-    ring = RingSum(part_image, relay, out, inbox, send, recv, 21)
+    ring = RingSum(part_image, relay, out, inbox, send, recv, 33)
     ring.start()
-    sums.forward(0)
+    for total in sums:
+        total.forward(0)
     ring.forward()
-    sums.forward(1)
-    sums.forward(2)
+    for step in (1, 2):
+        for total in sums:
+            total.forward(step)
     ring.finish(image_sum)
-    sums.finish(text_sum)
+    for total, rows in zip(sums, HALVES):
+        total.finish(text_sum.at[rows])
 
 
 def exchange(value, mask, beside):
@@ -492,7 +516,7 @@
     total = pltpu.VMEM((TILE, WIDTH), jnp.float32)
 
     own = call(prepare, "prepare", None, bf16(2, ROWS, WIDTH), [])(image, text)
-    scratch = [*semaphores(12), pltpu.SemaphoreType.DMA((2,))]
+    scratch = [*semaphores(18), pltpu.SemaphoreType.DMA((2,))]
     beside = call(gather, "gather", 0, (stack, stack), scratch)
     one, (own_images, own_texts) = exchange(own, masks[0], beside)(own)
     two, (one_images, one_texts) = exchange(own, masks[1], beside)(one)
@@ -507,7 +531,7 @@
             pltpu.VMEM((SIDE, 1, ROWS), jnp.int32),
             *RING_SUM,
             *CHAIN_SUM,
-            *semaphores(27),
+            *semaphores(39),
             pltpu.SemaphoreType.DMA((3,)),
         ],
         flops=24 * TILE * TILE * WIDTH,

time: 122 us -> 135 us (1.11)
  Pallas kernels: 96.2 us -> 113 us
  starting transfers between devices: 17.8 us -> 14.9 us
    pallas_call x5, Pallas kernels: 96.2 us -> 113 us  [run(): pl.pallas_call(kernel, out_shape=out, in_specs=specs or [VMEM] * len(args...]
    ppermute x2, starting transfers between devices: 17.8 us -> 14.9 us  [branch(): return lambda v, w: (lax.ppermute(v, 'blk', pairs), beside(w))]
  transfers between devices with their start and end apart: 2 -> 2, of which waited for: 0 -> 0; matrix products, arithmetic and copies ran while one was open for 0% -> 0% of each run, Pallas kernels for 47% -> 53%
where the time goes in v2:
time: 135 us
  Pallas kernels  113 us (84%)
  starting transfers between devices  14.9 us (11%)
  local copies, waits for them, and re-layouts  3.53 us (3%)
  between operations  3.29 us (2%)
    pallas_call x5, Pallas kernels, run(): pl.pallas_call(kernel, out_shape=out, in_specs=specs or [VMEM] * len(args...  113 us
    ppermute x2, starting transfers between devices, branch(): return lambda v, w: (lax.ppermute(v, 'blk', pairs), beside(w))  14.9 us
    unnamed x12, local copies, waits for them, and re-layouts  3.02 us
  transfers between devices with their start and end apart: 2, of which 0 were waited for; matrix products, arithmetic and copies ran while one was open for 0% of the time, Pallas kernels for 53%

profile of v2, /device:TPU:64, one launch (start us, length us, event | category | flops | bytes accessed | tf_op | source)
XLA Modules:
  0.0 135.0 jit_solution(13463852546795656666)
XLA Ops:
  0.6 0.0 copy-start
  0.6 0.9 copy-done
  1.6 0.0 copy-start.2
  1.6 0.9 copy-done.2
  2.5 0.0 copy-start.5
  2.5 0.2 prepare.1
  2.7 0.5 copy-done.5
  3.2 0.5 fusion
  4.4 44.3 %conditional.2 = (bf16[2,96,1152]{2,1,0:T(8,128)(2,1)}, bf16[4,96,1152]{2,1,0:T(8,128)(2,1)S(1)}, bf16[4,96,1152]{2,1,0:T(8,128)(2,1)S(1)}) conditional(s32[]{:T(128)} %bitcast, bf16[2,96,1152]{2,1,0:T(8,128)(2,1)S(1)} %prepare.1, bf16[2,96,1152]{2,1,0:T(8,128)(2,1)S(1)} %prepare.1, ...), branch_computations={%region_0.0_spmd, %region_1.0_spmd, %region_2.0_spmd, %region_3.0_... | conditional | bytes 35323968 | solution.py:485
  4.4 9.5 %collective-permute-start.16 = (bf16[2,96,1152]{2,1,0:T(8,128)(2,1)S(1)}, bf16[2,96,1152]{2,1,0:T(8,128)(2,1)}, u32[]{:S(2)}, u32[]{:S(2)}) collective-permute-start(bf16[2,96,1152]{2,1,0:T(8,128)(2,1)S(1)} %pair.16), channel_id=1, source_target_pairs={{0,272},{16,256},{32,304},{48,288},{64,336},{80,320},{96,368},{112... | collective-permute-start | bytes 1327112 | tf_op jit(solution)/shard_map/cond/branch_16_fun/ppermute | solution.py:482
  13.9 34.6 %gather.78 = (bf16[4,96,1152]{2,1,0:T(8,128)(2,1)S(1)}, bf16[4,96,1152]{2,1,0:T(8,128)(2,1)S(1)}) custom-call(bf16[2,96,1152]{2,1,0:T(8,128)(2,1)S(1)} %pair.16), custom_call_target="tpu_custom_call" | custom-call | bytes 33554432 | tf_op jit(solution)/shard_map/cond/branch_16_fun/gather/pallas_call | solution.py:303
  48.5 0.0 collective-permute-done.16
  49.3 42.5 %conditional.3 = (bf16[2,96,1152]{2,1,0:T(8,128)(2,1)}, bf16[4,96,1152]{2,1,0:T(8,128)(2,1)S(1)}, bf16[4,96,1152]{2,1,0:T(8,128)(2,1)}) conditional(s32[]{:T(128)} %bitcast.1, (bf16[2,96,1152]{2,1,0:T(8,128)(2,1)S(1)}, bf16[2,96,1152]{2,1,0:T(8,128)(2,1)}) %tuple.255, (bf16[2,96,1152]{2,1,0:T(8,128)(2,1)S(1)}, ...), branch_computations={%region_31.0_spmd, %region_32.0_spmd, %region_33.0_spmd, %region_3... | conditional | bytes 35323968 | solution.py:485
  49.4 5.5 %collective-permute-start.60 = (bf16[2,96,1152]{2,1,0:T(8,128)(2,1)S(1)}, bf16[2,96,1152]{2,1,0:T(8,128)(2,1)}, u32[]{:S(2)}, u32[]{:S(2)}) collective-permute-start(bf16[2,96,1152]{2,1,0:T(8,128)(2,1)S(1)} %get-tuple-element.333), channel_id=1, source_target_pairs={{0,480},{16,496},{32,448},{48,464},{64,416},{80,432},{96,384},{112... | collective-permute-start | bytes 1327112 | tf_op jit(solution)/shard_map/cond/branch_29_fun/ppermute | solution.py:482
  54.8 36.7 %gather.122 = (bf16[4,96,1152]{2,1,0:T(8,128)(2,1)S(1)}, bf16[4,96,1152]{2,1,0:T(8,128)(2,1)}) custom-call(bf16[2,96,1152]{2,1,0:T(8,128)(2,1)} %get-tuple-element.334.pair), custom_call_target="tpu_custom_call" | custom-call | bytes 33554432 | tf_op jit(solution)/shard_map/cond/branch_29_fun/gather/pallas_call | solution.py:303
  91.6 0.0 collective-permute-done.60
  93.1 0.1 pad_maximum_fusion.scalars
  93.2 0.0 copy-start.4
  93.2 0.7 copy-done.4
  93.8 0.0 copy-start.1
  93.8 0.0 copy-start.3
  93.8 39.5 %core.1 = (f32[96,1152]{1,0:T(8,128)S(1)}, f32[96,1152]{1,0:T(8,128)S(1)}) custom-call(f32[2]{0:T(128)S(1)} %pad_maximum_fusion.scalars, bf16[4,96,1152]{2,1,0:T(8,128)(2,1)S(1)} %get-tuple-element.351.own_images, bf16[4,96,1152]{2,1,0:T(8,128)(2,1)S(1)} %get-tuple-element.352.own_texts, bf16[4,96,1152]{2,1,0:T(8,128)(2,1)S(1)} %get-tuple-element.354.one_images, ...), custom_call_target="tpu_custom_call" | custom-call | flops 4076863488 | bytes 33554432 | tf_op jit(solution)/shard_map/core/pallas_call | solution.py:303
  133.4 0.0 copy-done.1
  133.4 0.0 copy-done.3
  133.4 1.6 %conclude.1 = (bf16[96,1152]{1,0:T(8,128)(2,1)}, bf16[96,1152]{1,0:T(8,128)(2,1)}) custom-call(f32[2]{0:T(128)S(1)} %pad_maximum_fusion.scalars, bf16[96,1152]{1,0:T(8,128)(2,1)S(1)} %copy-done.1, bf16[96,1152]{1,0:T(8,128)(2,1)S(1)} %copy-done.3, f32[96,1152]{1,0:T(8,128)S(1)} %get-tuple-element.357.image_sum, f32[96,1152]{1,0:T(8,128)S(1)} %get-tuple-element.358.text_sum), custom_call_target="tpu_custom_call" | custom-call | bytes 33554432 | tf_op jit(solution)/shard_map/conclude/pallas_call | solution.py:303
Async XLA Ops:
  0.6 0.9 copy-start
  1.6 0.9 copy-start.2
  2.5 0.7 copy-start.5
  4.4 44.1 %collective-permute-start.16 = (bf16[2,96,1152]{2,1,0:T(8,128)(2,1)S(1)}, bf16[2,96,1152]{2,1,0:T(8,128)(2,1)}, u32[]{:S(2)}, u32[]{:S(2)}) collective-permute-start(bf16[2,96,1152]{2,1,0:T(8,128)(2,1)S(1)} %pair.16), channel_id=1, source_target_pairs={{0,272},{16,256},{32,304},{48,288},{64,336},{80,320},{96,368},{112... | collective-permute-start | bytes 1327112 | tf_op jit(solution)/shard_map/cond/branch_16_fun/ppermute | solution.py:482
  49.4 42.2 %collective-permute-start.60 = (bf16[2,96,1152]{2,1,0:T(8,128)(2,1)S(1)}, bf16[2,96,1152]{2,1,0:T(8,128)(2,1)}, u32[]{:S(2)}, u32[]{:S(2)}) collective-permute-start(bf16[2,96,1152]{2,1,0:T(8,128)(2,1)S(1)} %get-tuple-element.333), channel_id=1, source_target_pairs={{0,480},{16,496},{32,448},{48,464},{64,416},{80,432},{96,384},{112... | collective-permute-start | bytes 1327112 | tf_op jit(solution)/shard_map/cond/branch_29_fun/ppermute | solution.py:482
  93.2 0.7 copy-start.4
  93.8 39.5 %copy-start.1 = (bf16[96,1152]{1,0:T(8,128)(2,1)S(1)}, bf16[96,1152]{1,0:T(8,128)(2,1)}, u32[]{:S(2)}) copy-start(bf16[96,1152]{1,0:T(8,128)(2,1)} %image.3) | copy-start | bytes 663556
  93.8 39.5 %copy-start.3 = (bf16[96,1152]{1,0:T(8,128)(2,1)S(1)}, bf16[96,1152]{1,0:T(8,128)(2,1)}, u32[]{:S(2)}) copy-start(bf16[96,1152]{1,0:T(8,128)(2,1)} %text.3) | copy-start | bytes 663556
